TPU v7x, 128 devices: a whole 4x4x4 slice. The times are simulated.
128 devices in a mesh: dyn: 32 (over y, x, core), rad: 4 (over z).
Axes of the slice: x: 4, y: 4, z: 4, core: 2. Of those that a mesh axis runs over, the one named last changes fastest.
Arguments:
- thermal_profile: float32 [137, 262144], P(None, ('dyn', 'rad')), may hold values from 0.6 to 1.4
- gas_loadings: float32 [4, 137, 262144], P(None, None, ('dyn', 'rad')), may hold values from 0.05 to 2
- profile_footprint: float32 [262144], P(('dyn', 'rad')), may hold values from 1 to 4
- profile_segment: int32 [262144], P(('dyn', 'rad')), may hold values from 0 to 511
- segment_holder_chip: int32 [65536, 1], P(('dyn', 'rad')), may hold values from 0 to 127; in each aligned block of 512 rows (0 to 511, 512 to 1023, ...) at most 8 rows name the same one
- segment_box_local: int32 [65536], P(('dyn', 'rad')), may hold values from 0 to 255
- opacity_table: float32 [32, 4], replicated, may hold values from 0.002 to 0.5
- blackbody_fraction: float32 [32], replicated, may hold values from 0.02 to 0.1
Outputs:
- heating: float32 [137, 262144], P(None, ('dyn', 'rad'))
Inputs may be any that keep to these rules, and one draw needn't show every extreme that they name: `segment_holder_chip`: among the 512 pieces of one device, at most 8 name the same owner device.
All inputs are finite; a program needn't handle non-finite values.
Results may differ from a plain program's by a relative error of at most 0.0003.
Values sent between devices are 32-bit elements; how exact they have to be, the bound alone decides.
No kernel may reach another device: no remote copies, remote signals or barrier semaphores. Data moves between devices by JAX's collectives and lax.ppermute only.
A program may use at most 128 MiB of HBM per device.

v0:
```python
import functools

import jax
import jax.numpy as jnp
from jax import lax
from jax.experimental import pallas as pl
from jax.experimental.pallas import tpu as pltpu
from jax.sharding import PartitionSpec as P

AXES = ("dyn", "rad")
CAP = 8
LANES = 128
BF = jnp.bfloat16
F32 = jnp.float32
NT = (((1,), (1,)), ((), ()))
NN = (((1,), (0,)), ((), ()))
VMEM_LIMIT = 56 * 1024 * 1024


def up_to(value, step):
    return -(-value // step) * step


def parts_of(value, count):
    out = []
    for _ in range(count - 1):
        part = value.astype(BF)
        out.append(part)
        value = value - part.astype(F32)
    out.append(value.astype(BF))
    return out


def mask_to(mask):
    return jnp.where(mask, 1.0, 0.0).astype(BF)


def dot(a, b, dims):
    return lax.dot_general(a, b, dims, preferred_element_type=F32)


def slots_of(target, devices):
    pieces = target.shape[1]
    column = jnp.transpose(jnp.broadcast_to(target, (LANES, pieces)))
    ranks = []
    for j in range(pieces // LANES):
        part = target[:, j * LANES : (j + 1) * LANES]
        before = lax.broadcasted_iota(jnp.int32, (pieces, LANES), 0)
        me = lax.broadcasted_iota(jnp.int32, (pieces, LANES), 1) + j * LANES
        hit = (column == part) & (before < me)
        ranks.append(jnp.sum(jnp.where(hit, 1, 0), axis=0, keepdims=True))
    return jnp.concatenate(ranks, axis=1)


def slot_rows(target, rank, devices, store):
    pieces = target.shape[1]
    owner = lax.broadcasted_iota(jnp.int32, (devices, pieces), 0) == target
    for s in range(CAP):
        store(s, mask_to(owner & (rank == s)))


def piece_rows(segment, pieces):
    return mask_to(lax.broadcasted_iota(jnp.int32, (pieces, segment.shape[1]), 0) == segment)


class Plan:
    def __init__(self, fields, width):
        self.fields = fields
        self.whole = fields // LANES
        self.rest = fields - self.whole * LANES
        self.width = width
        self.tail = up_to(CAP * width, LANES) // LANES
        self.rows = CAP * self.whole + self.tail

    def spans(self, s):
        start = s * self.width
        first, shift = start // LANES, start % LANES
        yield first, shift, None if shift + self.width <= LANES else "low"
        if shift + self.width > LANES:
            yield first + 1, shift, "high"

    def pack(self, rests):
        lane = lax.broadcasted_iota(jnp.int32, rests[0].shape, 1)
        tiles = [None] * self.tail
        for s, rest in enumerate(rests):
            for tile, shift, side in self.spans(s):
                part = pltpu.roll(rest, shift, 1) if shift else rest
                if side == "low":
                    part = jnp.where(lane >= shift, part, 0.0)
                if side == "high":
                    part = jnp.where(lane < shift, part, 0.0)
                tiles[tile] = part if tiles[tile] is None else tiles[tile] + part
        return tiles

    def unpack(self, tiles, s):
        spans = list(self.spans(s))
        value, shift = tiles[spans[0][0]], spans[0][1]
        if len(spans) == 2:
            lane = lax.broadcasted_iota(jnp.int32, value.shape, 1)
            value = jnp.where(lane >= shift, value, tiles[spans[1][0]])
        return pltpu.roll(value, LANES - shift, 1) if shift else value


def gather_kernel(plan, devices, thermal, gas, weight, segment, target, box, out, rank_out, buf, sems, left, ones, comp, slot, wide):
    species, levels = buf.shape[0], buf.shape[1]
    pieces = target.shape[1]
    block = up_to(levels, 16)
    copies = [pltpu.make_async_copy(thermal, buf.at[0], sems.at[0])]
    copies += [pltpu.make_async_copy(gas.at[k], buf.at[k + 1], sems.at[k + 1]) for k in range(species - 1)]
    for copy in copies:
        copy.start()
    owner = target[...]
    rank = slots_of(owner, devices)
    rank_out[...] = rank

    def store(s, value):
        slot[s * devices : (s + 1) * devices, :] = value

    slot_rows(owner, rank, devices, store)
    ones[...] = piece_rows(segment[...], pieces)
    w = weight[...]
    high, low = parts_of(jnp.broadcast_to(w, (8, w.shape[1])), 2)
    left[2 * species * block :, :] = jnp.concatenate([high.astype(F32), low.astype(F32)], axis=0).astype(BF)
    for k in range(species):
        copies[k].wait()
        high, low = parts_of(buf[k] * w, 2)
        left[k * block : k * block + levels, :] = high
        left[(species + k) * block : (species + k) * block + levels, :] = low
    sums = dot(left[...], ones[...], NT)
    for k in range(species):
        a = k * block
        b = (species + k) * block
        comp[k * levels : (k + 1) * levels, :] = sums[a : a + levels] + sums[b : b + levels]
    total = species * levels
    end = 2 * species * block
    comp[total : total + 1, :] = sums[end : end + 1] + sums[end + 8 : end + 9]
    comp[total + 1 : total + 2, :] = box[...].astype(F32)
    comp[total + 2 :, :] = jnp.zeros((comp.shape[0] - total - 2, pieces), F32)
    acc = None
    for part in parts_of(comp[...], 3):
        term = dot(slot[...], part, NT)
        acc = term if acc is None else acc + term
    wide[...] = acc
    for k in range(plan.whole):
        for s in range(CAP):
            out[pl.ds(CAP * k + s, devices, stride=plan.rows), :] = wide[
                s * devices : (s + 1) * devices, k * LANES : (k + 1) * LANES
            ]
    rests = [wide[s * devices : (s + 1) * devices, plan.whole * LANES :] for s in range(CAP)]
    for j, tile in enumerate(plan.pack(rests)):
        out[pl.ds(CAP * plan.whole + j, devices, stride=plan.rows), :] = tile


def sweep(mean, t4, opacity, fraction, heat, lost, gain, levels, cells):
    points = opacity.shape[1]
    rate = [-opacity[a] for a in range(opacity.shape[0])]
    frac = fraction[...]

    def row(ref, index):
        return ref[pl.ds(index, 1), :]

    def down(l, flux):
        tau = rate[0] * row(mean, levels + l)
        for a in range(1, len(rate)):
            tau = tau + rate[a] * row(mean, (a + 1) * levels + l)
        take = 1.0 - jnp.exp(tau)
        lost[l] = take
        step = take * (frac * row(t4, l) - flux)
        gain[l] = jnp.sum(step.reshape(points // 8, 8, cells), axis=0)
        return flux + step

    bottom = lax.fori_loop(0, levels, down, jnp.zeros((points, cells), F32), unroll=8)
    surface = 0.95 * (frac * t4[levels - 1 : levels, :]) + 0.05 * bottom

    def up(i, flux):
        l = levels - 1 - i
        step = lost[l] * (frac * row(t4, l) - flux)
        part = gain[l] + jnp.sum(step.reshape(points // 8, 8, cells), axis=0)
        heat[pl.ds(l, 1), :] = -jnp.sum(part, axis=0, keepdims=True)
        return flux + step

    lax.fori_loop(0, levels, up, surface, unroll=8)


def radiate_kernel(plan, back, devices, levels, cells, arrived, opacity, fraction, out, parts, match, mean, t4, heat, lost, gain):
    fields = plan.fields
    lane = plan.rest
    tails = [arrived[pl.ds(CAP * plan.whole + j, devices, stride=plan.rows), :] for j in range(plan.tail)]
    pick = mask_to(lax.broadcasted_iota(jnp.int32, (8, LANES), 1) == lane - 1)
    rows = []
    for s in range(CAP):
        own = slice(s * devices, (s + 1) * devices)
        for k in range(plan.whole):
            value = arrived[pl.ds(CAP * k + s, devices, stride=plan.rows), :]
            for n, part in enumerate(parts_of(value, 3)):
                parts[n, own, k * LANES : (k + 1) * LANES] = part
        rest = plan.unpack(tails, s)
        split = parts_of(rest, 3)
        for n, part in enumerate(split):
            parts[n, own, plan.whole * LANES :] = part
        cell = rest[:, lane - 1 : lane].astype(jnp.int32)
        match[own, :] = mask_to(cell == lax.broadcasted_iota(jnp.int32, (devices, cells), 1))
        rows.append(dot(pick, split[0], NT)[0:1])
    cell_row = jnp.concatenate(rows, axis=1).astype(jnp.int32)
    slots = cell_row.shape[1]
    turned = mask_to(lax.broadcasted_iota(jnp.int32, (cells, slots), 0) == cell_row)
    acc = None
    for n in range(3):
        term = dot(turned, parts[n], NN)
        acc = term if acc is None else acc + term
    sums = jnp.transpose(acc)
    weight = sums[fields - 2 : fields - 1, :]
    mean[...] = sums[0 : mean.shape[0]] * (1.0 / jnp.maximum(weight, 1.0))
    square = mean[0:levels, :] * mean[0:levels, :]
    t4[0:levels, :] = square * square
    heat[levels:, :] = jnp.zeros((heat.shape[0] - levels, cells), F32)
    sweep(mean, t4, opacity, fraction, heat, lost, gain, levels, cells)
    acc = None
    for part in parts_of(heat[...], 3):
        term = dot(match[...], part, NT)
        acc = term if acc is None else acc + term
    for s in range(CAP):
        out[pl.ds(s, devices, stride=back.rows), :] = acc[s * devices : (s + 1) * devices, :LANES]
    rests = [acc[s * devices : (s + 1) * devices, LANES:] for s in range(CAP)]
    for j, tile in enumerate(back.pack(rests)):
        out[pl.ds(CAP + j, devices, stride=back.rows), :] = tile


def spread_kernel(back, devices, levels, returned, segment, target, rank, out, slot, wide):
    pieces = target.shape[1]

    def store(s, value):
        slot[s * devices : (s + 1) * devices, :] = value

    slot_rows(target[...], rank[...], devices, store)
    ones = piece_rows(segment[...], pieces)
    tails = [returned[pl.ds(CAP + j, devices, stride=back.rows), :] for j in range(back.tail)]
    for s in range(CAP):
        own = slice(s * devices, (s + 1) * devices)
        wide[own, :LANES] = returned[pl.ds(s, devices, stride=back.rows), :]
        wide[own, LANES:] = back.unpack(tails, s)
    turned = jnp.transpose(wide[...])[: up_to(levels, 16)]
    held = None
    for part in parts_of(turned, 3):
        term = dot(part, slot[...], NN)
        held = term if held is None else held + term
    acc = None
    for part in parts_of(held, 3):
        term = dot(part, ones, NN)
        acc = term if acc is None else acc + term
    out[...] = acc[:levels]


def shards(thermal, gas, footprint, segment, holder, box, opacity, fraction):
    levels, columns = thermal.shape
    species = gas.shape[0] + 1
    pieces = box.shape[0]
    points = fraction.shape[0]
    devices = lax.axis_size(AXES)
    cells = columns // 8
    slots = devices * CAP
    fields = species * levels + 2
    plan = Plan(fields, up_to(fields % LANES, 16))
    back = Plan(levels, up_to(levels % LANES, 16))
    padded = (plan.whole + 1) * LANES
    block = up_to(levels, 16)
    weight_row = footprint.reshape(1, columns)
    segment_row = segment.reshape(1, columns)
    target_row = holder.reshape(1, pieces)
    box_row = box.reshape(1, pieces)
    vmem = pl.BlockSpec(memory_space=pltpu.VMEM)
    hbm = pl.BlockSpec(memory_space=pl.ANY)
    params = pltpu.CompilerParams(vmem_limit_bytes=VMEM_LIMIT)

    outgoing, rank = pl.pallas_call(
        functools.partial(gather_kernel, plan, devices),
        out_shape=(
            jax.ShapeDtypeStruct((devices * plan.rows, LANES), F32),
            jax.ShapeDtypeStruct((1, pieces), jnp.int32),
        ),
        in_specs=[hbm, hbm, vmem, vmem, vmem, vmem],
        out_specs=(vmem, vmem),
        scratch_shapes=[
            pltpu.VMEM((species, levels, columns), F32),
            pltpu.SemaphoreType.DMA((species,)),
            pltpu.VMEM((2 * species * block + 16, columns), BF),
            pltpu.VMEM((pieces, columns), BF),
            pltpu.VMEM((padded, pieces), F32),
            pltpu.VMEM((slots, pieces), BF),
            pltpu.VMEM((slots, padded), F32),
        ],
        compiler_params=params,
        name="gather_pieces",
    )(thermal, gas, weight_row, segment_row, target_row, box_row)

    arrived = lax.all_to_all(
        outgoing.reshape(devices, 1, plan.rows * LANES), AXES, split_axis=0, concat_axis=0, tiled=True
    ).reshape(devices * plan.rows, LANES)

    heat_out = pl.pallas_call(
        functools.partial(radiate_kernel, plan, back, devices, levels, cells),
        out_shape=jax.ShapeDtypeStruct((devices * back.rows, LANES), F32),
        in_specs=[vmem, vmem, vmem],
        out_specs=vmem,
        scratch_shapes=[
            pltpu.VMEM((3, slots, padded), BF),
            pltpu.VMEM((slots, cells), BF),
            pltpu.VMEM((up_to(species * levels, 8), cells), F32),
            pltpu.VMEM((up_to(levels, 8), cells), F32),
            pltpu.VMEM((2 * LANES, cells), F32),
            pltpu.VMEM((levels, points, cells), F32),
            pltpu.VMEM((levels, 8, cells), F32),
        ],
        compiler_params=params,
        name="radiate_cells",
    )(
        arrived,
        jnp.broadcast_to(opacity.T[:, :, None], (species - 1, points, cells)),
        jnp.broadcast_to(fraction[:, None], (points, cells)),
    )

    returned = lax.all_to_all(
        heat_out.reshape(devices, 1, back.rows * LANES), AXES, split_axis=0, concat_axis=0, tiled=True
    ).reshape(devices * back.rows, LANES)

    return pl.pallas_call(
        functools.partial(spread_kernel, back, devices, levels),
        out_shape=jax.ShapeDtypeStruct((levels, columns), F32),
        in_specs=[vmem, vmem, vmem, vmem],
        out_specs=vmem,
        scratch_shapes=[
            pltpu.VMEM((slots, pieces), BF),
            pltpu.VMEM((slots, 2 * LANES), F32),
        ],
        compiler_params=params,
        name="spread_heat",
    )(returned, segment_row, target_row, rank)


def solution(mesh):
    placed = (
        P(None, AXES),
        P(None, None, AXES),
        P(AXES),
        P(AXES),
        P(AXES, None),
        P(AXES),
        P(),
        P(),
    )
    return jax.shard_map(shards, mesh=mesh, in_specs=placed, out_specs=P(None, AXES), check_vma=False)
```

profile of v0, /device:TPU:1, one launch (start us, length us, event | category | flops | bytes accessed | tf_op | source)
XLA Modules:
  0.0 104.1 jit_solution(17781792999733303267)
XLA Ops:
  0.0 7.0 %copy.10.gas = f32[4,137,2048]{2,1,0:T(8,128)} copy(f32[4,137,2048]{2,0,1:T(4,128)} %param.9) | data formatting | bytes 8978432 | tf_op args[1]
  7.0 12.2 %gather_pieces.1 = (f32[5504,128]{1,0:T(8,128)}, s32[1,512]{1,0:T(1,128)}) custom-call(f32[137,2048]{1,0:T(8,128)} %thermal.1, f32[4,137,2048]{2,1,0:T(8,128)} %copy.10.gas, f32[1,2048]{1,0:T(1,128)} %bitcast.17, s32[1,2048]{1,0:T(1,128)} %bitcast.13, s32[1,512]{1,0:T(1,128)} %bitcast.15, s32[1,512]{1,0:T(1,128)} %bitcast.18), custom_call_target="tpu_custom_call" | custom-call | tf_op jit(solution)/shard_map/gather_pieces/pallas_call | solution.py:275
  19.2 0.0 copy-start
  19.2 0.0 copy-start.1
  19.2 49.8 %all_to_all.10 = f32[128,1,5504]{2,1,0:T(1,128)} all-to-all(f32[128,1,5504]{2,1,0:T(1,128)} %bitcast.10), channel_id=1, replica_groups=mesh['dyn'=32,'rad'=4] {'dyn','rad'}, dimensions={0} | all-to-all | bytes 5636096 | tf_op jit(solution)/shard_map/all_to_all | solution.py:296
  69.0 0.0 copy-done
  69.0 0.7 broadcast_in_dim.4.opacity
  69.8 0.0 copy-done.1
  69.8 0.7 broadcast_in_dim.5.fraction
  70.5 10.1 %radiate_cells.1 = f32[1152,128]{1,0:T(8,128)} custom-call(f32[5504,128]{1,0:T(8,128)} %bitcast.9, f32[4,32,256]{2,1,0:T(8,128)} %broadcast_in_dim.4.opacity, f32[32,256]{1,0:T(8,128)} %broadcast_in_dim.5.fraction), custom_call_target="tpu_custom_call" | custom-call | tf_op jit(solution)/shard_map/radiate_cells/pallas_call | solution.py:300
  80.5 19.3 %all_to_all.11 = f32[128,1,1152]{2,1,0:T(1,128)} all-to-all(f32[128,1,1152]{2,1,0:T(1,128)} %bitcast.11), channel_id=1, replica_groups=mesh['dyn'=32,'rad'=4] {'dyn','rad'}, dimensions={0} | all-to-all | bytes 1179648 | tf_op jit(solution)/shard_map/all_to_all | solution.py:322
  99.8 4.3 %spread_heat.1 = f32[137,2048]{1,0:T(8,128)} custom-call(f32[1152,128]{1,0:T(8,128)} %bitcast.12, s32[1,2048]{1,0:T(1,128)} %bitcast.14, s32[1,512]{1,0:T(1,128)} %bitcast.16, s32[1,512]{1,0:T(1,128)} %get-tuple-element.8.rank), custom_call_target="tpu_custom_call" | custom-call | tf_op jit(solution)/shard_map/spread_heat/pallas_call | solution.py:326
Async XLA Ops:
  19.2 49.9 %copy-start = (f32[32,4]{0,1:T(4,128)S(1)}, f32[32,4]{0,1:T(4,128)}, u32[]{:S(2)}) copy-start(f32[32,4]{0,1:T(4,128)} %param.14) | copy-start | bytes 1540
  19.2 50.6 %copy-start.1 = (f32[32]{0:T(128)S(1)}, f32[32]{0:T(128)}, u32[]{:S(2)}) copy-start(f32[32]{0:T(128)} %param.15) | copy-start | bytes 388
where the time goes:
time: 105 us; the launch traced here: 104 us
  blocking collectives  69.2 us (66%)
  Pallas kernels  26.6 us (25%)
  local copies, waits for them, and re-layouts  8.4 us (8%)
    all_to_all x1, blocking collectives, shards(): lax.all_to_all(outgoing.reshape(devices, 1, plan.rows * LANES), AXES, spl...  49.8 us
    all_to_all x1, blocking collectives, shards(): lax.all_to_all(heat_out.reshape(devices, 1, back.rows * LANES), AXES, spl...  19.3 us
    pallas_call x1, Pallas kernels, shards(): pl.pallas_call(functools.partial(gather_kernel, plan, devices), out_shape...  12.2 us
    pallas_call x1, Pallas kernels, shards(): pl.pallas_call(functools.partial(radiate_kernel, plan, back, devices, lev...  10.1 us
    unnamed x5, local copies, waits for them, and re-layouts  7 us
    pallas_call x1, Pallas kernels, shards(): pl.pallas_call(functools.partial(spread_kernel, back, devices, levels), o...  4.3 us

commit v1 on v0

--- a/solution.py
+++ b/solution.py
@@ -14,7 +14,7 @@
 F32 = jnp.float32
 NT = (((1,), (1,)), ((), ()))
 NN = (((1,), (0,)), ((), ()))
-VMEM_LIMIT = 56 * 1024 * 1024
+MIB = 1024 * 1024
 
 
 def up_to(value, step):
@@ -101,60 +101,81 @@
         return pltpu.roll(value, LANES - shift, 1) if shift else value
 
 
-def gather_kernel(plan, devices, thermal, gas, weight, segment, target, box, out, rank_out, buf, sems, left, ones, comp, slot, wide):
-    species, levels = buf.shape[0], buf.shape[1]
+def gather_kernel(plan, devices, groups, thermal, gas, weight_in, segment_in, target_in, box_in, out, rank_out, buf, sems, weight, segment, target, box, left, ones, comp, slot):
+    species, levels, columns = buf.shape
     pieces = target.shape[1]
     block = up_to(levels, 16)
+    small = [(target_in, target), (segment_in, segment), (weight_in, weight), (box_in, box)]
+    rows = [pltpu.make_async_copy(a, b, sems.at[species + n]) for n, (a, b) in enumerate(small)]
+    for copy in rows:
+        copy.start()
     copies = [pltpu.make_async_copy(thermal, buf.at[0], sems.at[0])]
-    copies += [pltpu.make_async_copy(gas.at[k], buf.at[k + 1], sems.at[k + 1]) for k in range(species - 1)]
+    copies += [pltpu.make_async_copy(gas.at[:, k, :], buf.at[k + 1], sems.at[k + 1]) for k in range(species - 1)]
     for copy in copies:
         copy.start()
+    rows[0].wait()
     owner = target[...]
     rank = slots_of(owner, devices)
     rank_out[...] = rank
 
     def store(s, value):
-        slot[s * devices : (s + 1) * devices, :] = value
+        for n in range(2):
+            slot[s * devices : (s + 1) * devices, n * pieces : (n + 1) * pieces] = value
 
     slot_rows(owner, rank, devices, store)
-    ones[...] = piece_rows(segment[...], pieces)
+    rows[1].wait()
+    here = piece_rows(segment[...], pieces)
+    for n in range(2):
+        ones[:, n * columns : (n + 1) * columns] = here
+    rows[2].wait()
+    rows[3].wait()
     w = weight[...]
-    high, low = parts_of(jnp.broadcast_to(w, (8, w.shape[1])), 2)
-    left[2 * species * block :, :] = jnp.concatenate([high.astype(F32), low.astype(F32)], axis=0).astype(BF)
-    for k in range(species):
-        copies[k].wait()
-        high, low = parts_of(buf[k] * w, 2)
-        left[k * block : k * block + levels, :] = high
-        left[(species + k) * block : (species + k) * block + levels, :] = low
-    sums = dot(left[...], ones[...], NT)
-    for k in range(species):
-        a = k * block
-        b = (species + k) * block
-        comp[k * levels : (k + 1) * levels, :] = sums[a : a + levels] + sums[b : b + levels]
+    end = species * block
+    for n, part in enumerate(parts_of(jnp.broadcast_to(w, (16, columns)), 2)):
+        left[end:, n * columns : (n + 1) * columns] = part
     total = species * levels
-    end = 2 * species * block
-    comp[total : total + 1, :] = sums[end : end + 1] + sums[end + 8 : end + 9]
-    comp[total + 1 : total + 2, :] = box[...].astype(F32)
-    comp[total + 2 :, :] = jnp.zeros((comp.shape[0] - total - 2, pieces), F32)
-    acc = None
-    for part in parts_of(comp[...], 3):
-        term = dot(slot[...], part, NT)
-        acc = term if acc is None else acc + term
-    wide[...] = acc
-    for k in range(plan.whole):
-        for s in range(CAP):
-            out[pl.ds(CAP * k + s, devices, stride=plan.rows), :] = wide[
-                s * devices : (s + 1) * devices, k * LANES : (k + 1) * LANES
-            ]
-    rests = [wide[s * devices : (s + 1) * devices, plan.whole * LANES :] for s in range(CAP)]
-    for j, tile in enumerate(plan.pack(rests)):
-        out[pl.ds(CAP * plan.whole + j, devices, stride=plan.rows), :] = tile
-
-
-def sweep(mean, t4, opacity, fraction, heat, lost, gain, levels, cells):
-    points = opacity.shape[1]
-    rate = [-opacity[a] for a in range(opacity.shape[0])]
-    frac = fraction[...]
+    begin = 0
+    for group in groups:
+        for k in range(begin, begin + group):
+            copies[k].wait()
+            for n, part in enumerate(parts_of(buf[k] * w, 2)):
+                left[k * block : k * block + levels, n * columns : (n + 1) * columns] = part
+        stop = begin + group
+        last = stop == species
+        sums = dot(left[begin * block : left.shape[0] if last else stop * block, :], ones[...], NT)
+        for k in range(begin, stop):
+            a = (k - begin) * block
+            for n, part in enumerate(parts_of(sums[a : a + levels], 2)):
+                comp[k * levels : (k + 1) * levels, n * pieces : (n + 1) * pieces] = part
+        if last:
+            a = (stop - begin) * block
+            row = lax.broadcasted_iota(jnp.int32, (comp.shape[0] - total, pieces), 0)
+            rest = jnp.where(row == 0, sums[a : a + 1], jnp.where(row == 1, box[...].astype(F32), 0.0))
+            for n, part in enumerate(parts_of(rest, 2)):
+                comp[total:, n * pieces : (n + 1) * pieces] = part
+        begin = stop
+    wide = 2 * LANES
+    for k in range(comp.shape[0] // wide):
+        acc = dot(slot[...], comp[k * wide : (k + 1) * wide, :], NT)
+        for h in range(2):
+            tile = 2 * k + h
+            values = [acc[s * devices : (s + 1) * devices, h * LANES : (h + 1) * LANES] for s in range(CAP)]
+            if tile < plan.whole:
+                for s in range(CAP):
+                    out[pl.ds(CAP * tile + s, devices, stride=plan.rows), :] = values[s]
+            else:
+                for j, value in enumerate(plan.pack(values)):
+                    out[pl.ds(CAP * tile + j, devices, stride=plan.rows), :] = value
+
+
+def as_column(row, width):
+    n = row.shape[1]
+    same = lax.broadcasted_iota(jnp.int32, (n, n), 0) == lax.broadcasted_iota(jnp.int32, (n, n), 1)
+    return jnp.broadcast_to(jnp.sum(jnp.where(same, row, 0.0), axis=1, keepdims=True), (n, width))
+
+
+def sweep(mean, t4, rate, frac, heat, lost, gain, levels, cells):
+    points = frac.shape[0]
 
     def row(ref, index):
         return ref[pl.ds(index, 1), :]
@@ -182,7 +203,13 @@
     lax.fori_loop(0, levels, up, surface, unroll=8)
 
 
-def radiate_kernel(plan, back, devices, levels, cells, arrived, opacity, fraction, out, parts, match, mean, t4, heat, lost, gain):
+def radiate_kernel(plan, back, devices, levels, cells, arrived, opacity_in, fraction_in, out, opacity, fraction, sems, parts, match, mean, t4, heat, lost, gain):
+    copies = [
+        pltpu.make_async_copy(opacity_in, opacity, sems.at[0]),
+        pltpu.make_async_copy(fraction_in, fraction, sems.at[1]),
+    ]
+    for copy in copies:
+        copy.start()
     fields = plan.fields
     lane = plan.rest
     tails = [arrived[pl.ds(CAP * plan.whole + j, devices, stride=plan.rows), :] for j in range(plan.tail)]
@@ -214,7 +241,11 @@
     square = mean[0:levels, :] * mean[0:levels, :]
     t4[0:levels, :] = square * square
     heat[levels:, :] = jnp.zeros((heat.shape[0] - levels, cells), F32)
-    sweep(mean, t4, opacity, fraction, heat, lost, gain, levels, cells)
+    for copy in copies:
+        copy.wait()
+    rate = [as_column(-opacity[a : a + 1, :], cells) for a in range(opacity.shape[0])]
+    frac = as_column(fraction[...], cells)
+    sweep(mean, t4, rate, frac, heat, lost, gain, levels, cells)
     acc = None
     for part in parts_of(heat[...], 3):
         term = dot(match[...], part, NT)
@@ -251,58 +282,72 @@
     out[...] = acc[:levels]
 
 
-def shards(thermal, gas, footprint, segment, holder, box, opacity, fraction):
+VMEM = pl.BlockSpec(memory_space=pltpu.VMEM)
+HBM = pl.BlockSpec(memory_space=pl.ANY)
+
+
+def params(mib):
+    return pltpu.CompilerParams(vmem_limit_bytes=mib * MIB)
+
+
+def in_hbm(value):
+    return pltpu.with_memory_space_constraint(value, pltpu.HBM)
+
+
+def plans(levels, species):
+    fields = species * levels + 2
+    return Plan(fields, up_to(fields % LANES, 16)), Plan(levels, up_to(levels % LANES, 16))
+
+
+def gather_call(thermal, gas, weight_row, segment_row, target_row, box_row):
     levels, columns = thermal.shape
-    species = gas.shape[0] + 1
-    pieces = box.shape[0]
-    points = fraction.shape[0]
+    species = gas.shape[1] + 1
+    pieces = target_row.shape[1]
     devices = lax.axis_size(AXES)
-    cells = columns // 8
+    plan, _ = plans(levels, species)
+    padded = (plan.whole + 1) * LANES
     slots = devices * CAP
-    fields = species * levels + 2
-    plan = Plan(fields, up_to(fields % LANES, 16))
-    back = Plan(levels, up_to(levels % LANES, 16))
-    padded = (plan.whole + 1) * LANES
-    block = up_to(levels, 16)
-    weight_row = footprint.reshape(1, columns)
-    segment_row = segment.reshape(1, columns)
-    target_row = holder.reshape(1, pieces)
-    box_row = box.reshape(1, pieces)
-    vmem = pl.BlockSpec(memory_space=pltpu.VMEM)
-    hbm = pl.BlockSpec(memory_space=pl.ANY)
-    params = pltpu.CompilerParams(vmem_limit_bytes=VMEM_LIMIT)
-
-    outgoing, rank = pl.pallas_call(
-        functools.partial(gather_kernel, plan, devices),
+    return pl.pallas_call(
+        functools.partial(gather_kernel, plan, devices, (3, 2)),
         out_shape=(
             jax.ShapeDtypeStruct((devices * plan.rows, LANES), F32),
             jax.ShapeDtypeStruct((1, pieces), jnp.int32),
         ),
-        in_specs=[hbm, hbm, vmem, vmem, vmem, vmem],
-        out_specs=(vmem, vmem),
+        in_specs=[HBM] * 6,
+        out_specs=(VMEM, VMEM),
         scratch_shapes=[
             pltpu.VMEM((species, levels, columns), F32),
-            pltpu.SemaphoreType.DMA((species,)),
-            pltpu.VMEM((2 * species * block + 16, columns), BF),
-            pltpu.VMEM((pieces, columns), BF),
-            pltpu.VMEM((padded, pieces), F32),
-            pltpu.VMEM((slots, pieces), BF),
-            pltpu.VMEM((slots, padded), F32),
+            pltpu.SemaphoreType.DMA((species + 4,)),
+            pltpu.VMEM((1, columns), F32),
+            pltpu.VMEM((1, columns), jnp.int32),
+            pltpu.VMEM((1, pieces), jnp.int32),
+            pltpu.VMEM((1, pieces), jnp.int32),
+            pltpu.VMEM((species * up_to(levels, 16) + 16, 2 * columns), BF),
+            pltpu.VMEM((pieces, 2 * columns), BF),
+            pltpu.VMEM((padded, 2 * pieces), BF),
+            pltpu.VMEM((slots, 2 * pieces), BF),
         ],
-        compiler_params=params,
+        compiler_params=params(34),
         name="gather_pieces",
-    )(thermal, gas, weight_row, segment_row, target_row, box_row)
-
-    arrived = lax.all_to_all(
-        outgoing.reshape(devices, 1, plan.rows * LANES), AXES, split_axis=0, concat_axis=0, tiled=True
-    ).reshape(devices * plan.rows, LANES)
-
-    heat_out = pl.pallas_call(
+    )(*map(in_hbm, (thermal, gas, weight_row, segment_row, target_row, box_row)))
+
+
+def radiate_call(arrived, opacity, fraction, levels, cells):
+    absorbers, points = opacity.shape
+    species = absorbers + 1
+    devices = lax.axis_size(AXES)
+    plan, back = plans(levels, species)
+    padded = (plan.whole + 1) * LANES
+    slots = devices * CAP
+    return pl.pallas_call(
         functools.partial(radiate_kernel, plan, back, devices, levels, cells),
         out_shape=jax.ShapeDtypeStruct((devices * back.rows, LANES), F32),
-        in_specs=[vmem, vmem, vmem],
-        out_specs=vmem,
+        in_specs=[VMEM, HBM, HBM],
+        out_specs=VMEM,
         scratch_shapes=[
+            pltpu.VMEM((absorbers, points), F32),
+            pltpu.VMEM((1, points), F32),
+            pltpu.SemaphoreType.DMA((2,)),
             pltpu.VMEM((3, slots, padded), BF),
             pltpu.VMEM((slots, cells), BF),
             pltpu.VMEM((up_to(species * levels, 8), cells), F32),
@@ -311,30 +356,49 @@
             pltpu.VMEM((levels, points, cells), F32),
             pltpu.VMEM((levels, 8, cells), F32),
         ],
-        compiler_params=params,
+        compiler_params=params(28),
         name="radiate_cells",
-    )(
-        arrived,
-        jnp.broadcast_to(opacity.T[:, :, None], (species - 1, points, cells)),
-        jnp.broadcast_to(fraction[:, None], (points, cells)),
-    )
-
-    returned = lax.all_to_all(
-        heat_out.reshape(devices, 1, back.rows * LANES), AXES, split_axis=0, concat_axis=0, tiled=True
-    ).reshape(devices * back.rows, LANES)
-
+    )(arrived, in_hbm(opacity), in_hbm(fraction))
+
+
+def spread_call(returned, segment_row, target_row, rank, levels):
+    columns = segment_row.shape[1]
+    pieces = target_row.shape[1]
+    devices = lax.axis_size(AXES)
+    _, back = plans(levels, 1)
+    slots = devices * CAP
     return pl.pallas_call(
         functools.partial(spread_kernel, back, devices, levels),
         out_shape=jax.ShapeDtypeStruct((levels, columns), F32),
-        in_specs=[vmem, vmem, vmem, vmem],
-        out_specs=vmem,
+        in_specs=[VMEM, VMEM, VMEM, VMEM],
+        out_specs=VMEM,
         scratch_shapes=[
             pltpu.VMEM((slots, pieces), BF),
             pltpu.VMEM((slots, 2 * LANES), F32),
         ],
-        compiler_params=params,
+        compiler_params=params(20),
         name="spread_heat",
     )(returned, segment_row, target_row, rank)
+
+
+def exchange(value):
+    devices = lax.axis_size(AXES)
+    chunks = value.reshape(devices, 1, value.size // devices)
+    return lax.all_to_all(chunks, AXES, split_axis=0, concat_axis=0, tiled=True).reshape(value.shape)
+
+
+def shards(thermal, gas, footprint, segment, holder, box, opacity, fraction):
+    levels, columns = thermal.shape
+    pieces = box.shape[0]
+    segment_row = segment.reshape(1, columns)
+    target_row = holder.reshape(1, pieces)
+    outgoing, rank = gather_call(
+        thermal, gas.transpose(1, 0, 2), footprint.reshape(1, columns), segment_row, target_row, box.reshape(1, pieces)
+    )
+    arrived = exchange(outgoing)
+    heat = radiate_call(arrived, opacity.T, fraction.reshape(1, -1), levels, columns // 8)
+    returned = exchange(heat)
+    return spread_call(returned, segment_row, target_row, rank, levels)
 
 
 def solution(mesh):

time: 105 us -> 86.2 us (0.82)
  local copies, waits for them, and re-layouts: 8.4 us -> 0.01 us
  Pallas kernels: 26.6 us -> 18.4 us
  blocking collectives: 69.2 us -> 67.7 us
    pallas_call x3, Pallas kernels: 26.6 us -> 18.4 us  [the longest x1 7.82 us: gather_call(): pl.pallas_call(functools.partial(gather_kernel, plan, devices, (3, 2)), o...]
    unnamed x5 -> x4, local copies, waits for them, and re-layouts: 7 us -> 0.01 us
    all_to_all x2, blocking collectives: 69.2 us -> 67.7 us  [exchange(): lax.all_to_all(chunks, AXES, split_axis=0, concat_axis=0, tiled=True)]
    broadcast_in_dim x2 -> x0, local copies, waits for them, and re-layouts: 1.4 us -> none  [the longest x1 0.73 us: shards(): jnp.broadcast_to(opacity.T[:, :, None], (species - 1, points, cells))]
where the time goes in v1:
time: 86.2 us; the launch traced here: 86.1 us
  blocking collectives  67.7 us (79%)
  Pallas kernels  18.4 us (21%)
    all_to_all x2, blocking collectives, exchange(): lax.all_to_all(chunks, AXES, split_axis=0, concat_axis=0, tiled=True)  67.7 us
    pallas_call x1, Pallas kernels, gather_call(): pl.pallas_call(functools.partial(gather_kernel, plan, devices, (3, 2)), o...  7.82 us
    pallas_call x1, Pallas kernels, radiate_call(): pl.pallas_call(functools.partial(radiate_kernel, plan, back, devices, lev...  7.36 us
    pallas_call x1, Pallas kernels, spread_call(): pl.pallas_call(functools.partial(spread_kernel, back, devices, levels), o...  3.23 us

profile of v1, /device:TPU:1, one launch (start us, length us, event | category | flops | bytes accessed | tf_op | source)
XLA Modules:
  0.0 86.1 jit_solution(5067915115427833157)
XLA Ops:
  0.0 7.8 %gather_pieces.1 = (f32[5504,128]{1,0:T(8,128)S(1)}, s32[1,512]{1,0:T(1,128)S(1)}) custom-call(f32[137,2048]{1,0:T(8,128)} %thermal.1, f32[137,4,2048]{2,1,0:T(4,128)} %bitcast.19, f32[1,2048]{1,0:T(1,128)} %bitcast.20, s32[1,2048]{1,0:T(1,128)} %bitcast.15, s32[1,512]{1,0:T(1,128)} %bitcast.17, s32[1,512]{1,0:T(1,128)} %bitcast.21), custom_call_target="tpu_custom_call" | custom-call | tf_op jit(solution)/shard_map/gather_pieces/pallas_call | solution.py:310
  7.8 49.5 %all_to_all.10 = f32[128,1,5504]{2,1,0:T(1,128)S(1)} all-to-all(f32[128,1,5504]{2,1,0:T(1,128)S(1)} %bitcast.12), channel_id=1, replica_groups=mesh['dyn'=32,'rad'=4] {'dyn','rad'}, dimensions={0} | all-to-all | bytes 5636096 | tf_op jit(solution)/shard_map/all_to_all | solution.py:387
  57.3 0.0 copy-start
  57.4 0.0 copy-start.1
  57.4 7.4 %radiate_cells.1 = f32[1152,128]{1,0:T(8,128)S(1)} custom-call(f32[5504,128]{1,0:T(8,128)S(1)} %bitcast.11, f32[4,32]{1,0:T(4,128)} %bitcast.22, f32[1,32]{1,0:T(1,128)} %bitcast.23), custom_call_target="tpu_custom_call" | custom-call | tf_op jit(solution)/shard_map/radiate_cells/pallas_call | solution.py:342
  64.7 18.1 %all_to_all.11 = f32[128,1,1152]{2,1,0:T(1,128)S(1)} all-to-all(f32[128,1,1152]{2,1,0:T(1,128)S(1)} %bitcast.14), channel_id=1, replica_groups=mesh['dyn'=32,'rad'=4] {'dyn','rad'}, dimensions={0} | all-to-all | bytes 1179648 | tf_op jit(solution)/shard_map/all_to_all | solution.py:387
  82.9 0.0 copy-done
  82.9 0.0 copy-done.1
  82.9 3.2 %spread_heat.1 = f32[137,2048]{1,0:T(8,128)} custom-call(f32[1152,128]{1,0:T(8,128)S(1)} %bitcast.13, s32[1,2048]{1,0:T(1,128)S(1)} %bitcast.16, s32[1,512]{1,0:T(1,128)S(1)} %bitcast.18, s32[1,512]{1,0:T(1,128)S(1)} %get-tuple-element.8.rank), custom_call_target="tpu_custom_call" | custom-call | tf_op jit(solution)/shard_map/spread_heat/pallas_call | solution.py:370
Async XLA Ops:
  57.3 25.5 %copy-start = (s32[2048]{0:T(1024)S(1)}, s32[2048]{0:T(1024)}, u32[]{:S(2)}) copy-start(s32[2048]{0:T(1024)} %param.11) | copy-start | bytes 24580
  57.4 25.5 %copy-start.1 = (s32[512,1]{0,1:T(1,128)S(1)}, s32[512,1]{0,1:T(1,128)}, u32[]{:S(2)}) copy-start(s32[512,1]{0,1:T(1,128)} %param.12) | copy-start | bytes 6148

commit v2 on v1

v2 whole, which is shorter than its diff:
```python
import functools

import jax
import jax.numpy as jnp
from jax import lax
from jax.experimental import pallas as pl
from jax.experimental.pallas import tpu as pltpu
from jax.sharding import PartitionSpec as P

AXES = ("dyn", "rad")
CAP = 8
LANES = 128
BF = jnp.bfloat16
F32 = jnp.float32
NT = (((1,), (1,)), ((), ()))
NN = (((1,), (0,)), ((), ()))
MIB = 1024 * 1024
LEVELS = 16
LOG2E = 1.4426950408889634


def up_to(value, step):
    return -(-value // step) * step


def parts_of(value, count):
    out = []
    for _ in range(count - 1):
        part = value.astype(BF)
        out.append(part)
        value = value - part.astype(F32)
    out.append(value.astype(BF))
    return out


def mask_to(mask):
    return jnp.where(mask, 1.0, 0.0).astype(BF)


def dot(a, b, dims):
    return lax.dot_general(a, b, dims, preferred_element_type=F32)


def slots_of(target, devices):
    pieces = target.shape[1]
    column = jnp.transpose(jnp.broadcast_to(target, (LANES, pieces)))
    ranks = []
    for j in range(pieces // LANES):
        part = target[:, j * LANES : (j + 1) * LANES]
        before = lax.broadcasted_iota(jnp.int32, (pieces, LANES), 0)
        me = lax.broadcasted_iota(jnp.int32, (pieces, LANES), 1) + j * LANES
        hit = (column == part) & (before < me)
        ranks.append(jnp.sum(jnp.where(hit, 1, 0), axis=0, keepdims=True))
    return jnp.concatenate(ranks, axis=1)


def slot_rows(target, rank, devices, store):
    pieces = target.shape[1]
    owner = lax.broadcasted_iota(jnp.int32, (devices, pieces), 0) == target
    for s in range(CAP):
        store(s, mask_to(owner & (rank == s)))


def piece_rows(segment, pieces):
    return mask_to(lax.broadcasted_iota(jnp.int32, (pieces, segment.shape[1]), 0) == segment)


class Plan:
    def __init__(self, fields, width):
        self.fields = fields
        self.whole = fields // LANES
        self.rest = fields - self.whole * LANES
        self.width = width
        self.tail = up_to(CAP * width, LANES) // LANES
        self.rows = CAP * self.whole + self.tail

    def spans(self, s):
        start = s * self.width
        first, shift = start // LANES, start % LANES
        yield first, shift, None if shift + self.width <= LANES else "low"
        if shift + self.width > LANES:
            yield first + 1, shift, "high"

    def pack(self, rests):
        lane = lax.broadcasted_iota(jnp.int32, rests[0].shape, 1)
        tiles = [None] * self.tail
        for s, rest in enumerate(rests):
            for tile, shift, side in self.spans(s):
                part = pltpu.roll(rest, shift, 1) if shift else rest
                if side == "low":
                    part = jnp.where(lane >= shift, part, 0.0)
                if side == "high":
                    part = jnp.where(lane < shift, part, 0.0)
                tiles[tile] = part if tiles[tile] is None else tiles[tile] + part
        return tiles

    def unpack(self, tiles, s):
        spans = list(self.spans(s))
        value, shift = tiles[spans[0][0]], spans[0][1]
        if len(spans) == 2:
            lane = lax.broadcasted_iota(jnp.int32, value.shape, 1)
            value = jnp.where(lane >= shift, value, tiles[spans[1][0]])
        return pltpu.roll(value, LANES - shift, 1) if shift else value


def gather_kernel(plan, devices, groups, thermal, gas, weight_in, segment_in, target_in, box_in, out, ones, slot, buf, sems, weight, segment, target, box, left, comp):
    species, levels, columns = buf.shape
    pieces = target.shape[1]
    block = up_to(levels, 16)
    small = [(target_in, target), (segment_in, segment), (weight_in, weight), (box_in, box)]
    rows = [pltpu.make_async_copy(a, b, sems.at[species + n]) for n, (a, b) in enumerate(small)]
    for copy in rows:
        copy.start()
    copies = [pltpu.make_async_copy(thermal, buf.at[0], sems.at[0])]
    copies += [pltpu.make_async_copy(gas.at[:, k, :], buf.at[k + 1], sems.at[k + 1]) for k in range(species - 1)]
    for copy in copies:
        copy.start()
    rows[0].wait()
    owner = target[...]
    rank = slots_of(owner, devices)

    def store(s, value):
        slot[s * devices : (s + 1) * devices, :] = value

    slot_rows(owner, rank, devices, store)
    rows[1].wait()
    ones[...] = piece_rows(segment[...], pieces)
    rows[2].wait()
    rows[3].wait()
    w = weight[...]
    total = species * levels
    end = 2 * species * block
    pair = parts_of(jnp.broadcast_to(w, (8, columns)), 2)
    left[end:, :] = jnp.concatenate([part.astype(F32) for part in pair], axis=0).astype(BF)

    def load(k):
        copies[k].wait()
        for n, part in enumerate(parts_of(buf[k] * w, 2)):
            left[(2 * k + n) * block : (2 * k + n) * block + levels, :] = part

    def keep(first, rows, values):
        for n, part in enumerate(parts_of(values, 2)):
            comp[first : first + rows, n * pieces : (n + 1) * pieces] = part

    bounds = [sum(groups[:n]) for n in range(len(groups) + 1)]
    for begin, stop in zip(bounds, bounds[1:]):
        last = stop == species
        for k in range(begin, stop):
            load(k)
        sums = dot(left[2 * begin * block : end + 16 if last else 2 * stop * block, :], ones[...], NT)
        for k in range(begin, stop):
            a = 2 * (k - begin) * block
            keep(k * levels, levels, sums[a : a + levels] + sums[a + block : a + block + levels])
        if last:
            a = 2 * (stop - begin) * block
            row = lax.broadcasted_iota(jnp.int32, (comp.shape[0] - total, pieces), 0)
            held = sums[a : a + 1] + sums[a + 8 : a + 9]
            keep(total, comp.shape[0] - total, jnp.where(row == 0, held, jnp.where(row == 1, box[...].astype(F32), 0.0)))
    wide = 2 * LANES
    for k in range(comp.shape[0] // wide):
        pair = [comp[k * wide : (k + 1) * wide, n * pieces : (n + 1) * pieces] for n in range(2)]
        acc = dot(slot[...], pair[0], NT) + dot(slot[...], pair[1], NT)
        for h in range(2):
            tile = 2 * k + h
            values = [acc[s * devices : (s + 1) * devices, h * LANES : (h + 1) * LANES] for s in range(CAP)]
            if tile < plan.whole:
                for s in range(CAP):
                    out[pl.ds(CAP * tile + s, devices, stride=plan.rows), :] = values[s]
            else:
                for j, value in enumerate(plan.pack(values)):
                    out[pl.ds(CAP * tile + j, devices, stride=plan.rows), :] = value


def as_column(row, width):
    n = row.shape[1]
    same = lax.broadcasted_iota(jnp.int32, (n, n), 0) == lax.broadcasted_iota(jnp.int32, (n, n), 1)
    return jnp.broadcast_to(jnp.sum(jnp.where(same, row, 0.0), axis=1, keepdims=True), (n, width))


def depth_matrix(opacity, points):
    absorbers = opacity.shape[0]
    width = 4 * absorbers * LEVELS
    column = lax.broadcasted_iota(jnp.int32, (points, width), 1)
    held = jnp.zeros((points, width), F32)
    for a in range(absorbers):
        value = as_column(opacity[a : a + 1, :] * -LOG2E, width)
        for n, part in enumerate(parts_of(value, 2)):
            for m in range(2):
                held = jnp.where(column // LEVELS == (2 * n + m) * absorbers + a, part.astype(F32), held)
    level = lax.rem(column, LEVELS)
    return jnp.concatenate([jnp.where(level == i, held, 0.0) for i in range(LEVELS)], axis=0).astype(BF)


def sweep(depths, xs, t4, frac, lost, gain, levels, cells):
    points = frac.shape[0]
    halves = gain.shape[0]

    def fold(value):
        return jnp.sum(value.reshape(points // 8, 8, cells), axis=0)

    flux = jnp.zeros((points, cells), F32)
    for b in range(up_to(levels, LEVELS) // LEVELS):
        take = 1.0 - jnp.exp2(dot(depths, xs[b], NN))
        for i in range(min(LEVELS, levels - b * LEVELS)):
            l = b * LEVELS + i
            own = take[i * points : (i + 1) * points]
            lost[l] = own
            step = own * (frac * t4[l : l + 1, :] - flux)
            part = fold(step)
            for h in range(halves):
                gain[h, 8 * l : 8 * l + 8, :] = part[:, h * LANES : (h + 1) * LANES]
            flux = flux + step
    flux = 0.95 * (frac * t4[levels - 1 : levels, :]) + 0.05 * flux
    for l in range(levels - 1, -1, -1):
        step = lost[l] * (frac * t4[l : l + 1, :] - flux)
        part = fold(step)
        for h in range(halves):
            gain[h, 8 * l : 8 * l + 8, :] += part[:, h * LANES : (h + 1) * LANES]
        flux = flux + step


def radiate_kernel(plan, back, devices, levels, cells, arrived, opacity_in, fraction_in, out, opacity, fraction, sems, parts, match, mean, xs, t4, heat, lost, gain):
    copies = [
        pltpu.make_async_copy(opacity_in, opacity, sems.at[0]),
        pltpu.make_async_copy(fraction_in, fraction, sems.at[1]),
    ]
    for copy in copies:
        copy.start()
    fields = plan.fields
    lane = plan.rest
    slots = devices * CAP
    absorbers, points = opacity.shape
    tails = [arrived[pl.ds(CAP * plan.whole + j, devices, stride=plan.rows), :] for j in range(plan.tail)]
    pick = mask_to(lax.broadcasted_iota(jnp.int32, (8, LANES), 1) == lane - 1)
    rows = []
    for s in range(CAP):
        for k in range(plan.whole + 1):
            if k < plan.whole:
                value = arrived[pl.ds(CAP * k + s, devices, stride=plan.rows), :]
            else:
                value = plan.unpack(tails, s)
            split = parts_of(value, 2)
            for n, part in enumerate(split):
                first = n * slots + s * devices
                parts[first : first + devices, k * LANES : (k + 1) * LANES] = part
        cell = value[:, lane - 1 : lane].astype(jnp.int32)
        here = mask_to(cell == lax.broadcasted_iota(jnp.int32, (devices, cells), 1))
        for n in range(2):
            match[s * devices : (s + 1) * devices, n * cells : (n + 1) * cells] = here
        rows.append(dot(pick, split[0], NT)[0:1])
    cell_row = jnp.concatenate(rows, axis=1).astype(jnp.int32)
    turned = mask_to(lax.broadcasted_iota(jnp.int32, (cells, slots), 0) == cell_row)
    sums = jnp.transpose(dot(jnp.concatenate([turned, turned], axis=1), parts[...], NN))
    inverse = 1.0 / jnp.maximum(sums[fields - 2 : fields - 1, :], 1.0)
    warm = sums[0:levels] * inverse
    square = warm * warm
    t4[0:levels, :] = square * square
    block = mean.shape[0]
    mean[levels:, :] = jnp.zeros((block - levels, cells), F32)
    for a in range(absorbers):
        mean[0:levels, :] = sums[(a + 1) * levels : (a + 2) * levels] * inverse
        for n, part in enumerate(parts_of(mean[...], 2)):
            for m in range(2):
                first = ((2 * m + n) * absorbers + a) * LEVELS
                for b in range(block // LEVELS):
                    xs[b, first : first + LEVELS, :] = part[b * LEVELS : (b + 1) * LEVELS]
    for copy in copies:
        copy.wait()
    frac = as_column(fraction[...], cells)
    sweep(depth_matrix(opacity, points), xs, t4, frac, lost, gain, levels, cells)
    heat[...] = jnp.zeros(heat.shape, BF)
    for h in range(gain.shape[0]):
        total = gain[h, pl.ds(0, levels, stride=8), :]
        for g in range(1, 8):
            total = total + gain[h, pl.ds(g, levels, stride=8), :]
        for n, part in enumerate(parts_of(-total, 2)):
            first = n * cells + h * LANES
            heat[0:levels, first : first + LANES] = part
    acc = dot(match[...], heat[...], NT)
    for s in range(CAP):
        out[pl.ds(s, devices, stride=back.rows), :] = acc[s * devices : (s + 1) * devices, :LANES]
    rests = [acc[s * devices : (s + 1) * devices, LANES:] for s in range(CAP)]
    for j, tile in enumerate(back.pack(rests)):
        out[pl.ds(CAP + j, devices, stride=back.rows), :] = tile


def spread_kernel(back, devices, levels, chunks, returned, ones, slot, out, wide, held, sems):
    rows, columns = held.shape
    pieces = slot.shape[1]
    block = up_to(levels, 16)
    tails = [returned[pl.ds(CAP + j, devices, stride=back.rows), :] for j in range(back.tail)]
    for s in range(CAP):
        own = slice(s * devices, (s + 1) * devices)
        wide[own, :LANES] = returned[pl.ds(s, devices, stride=back.rows), :]
        wide[own, LANES:] = back.unpack(tails, s)
    turned = jnp.transpose(wide[...])[:block]
    both = dot(jnp.concatenate(parts_of(turned, 2), axis=0), slot[...], NN)
    both = jnp.concatenate(parts_of(both[:block] + both[block:], 2), axis=0)
    size = columns // chunks
    copies = []
    for c in range(chunks):
        own = slice(c * size, (c + 1) * size)
        value = dot(both, ones[:, own], NN)
        held[:, own] = value[:rows] + value[block : block + rows]
        copies.append(pltpu.make_async_copy(held.at[:, own], out.at[:, own], sems.at[c]))
        copies[-1].start()
    for copy in copies:
        copy.wait()


VMEM = pl.BlockSpec(memory_space=pltpu.VMEM)
HBM = pl.BlockSpec(memory_space=pl.ANY)


def params(mib):
    return pltpu.CompilerParams(vmem_limit_bytes=mib * MIB)


def in_hbm(value):
    return pltpu.with_memory_space_constraint(value, pltpu.HBM)


def plans(levels, species):
    fields = species * levels + 2
    return Plan(fields, up_to(fields % LANES, 16)), Plan(levels, up_to(levels % LANES, 16))


def gather_call(thermal, gas, weight_row, segment_row, target_row, box_row):
    levels, columns = thermal.shape
    species = gas.shape[1] + 1
    pieces = target_row.shape[1]
    devices = lax.axis_size(AXES)
    plan, _ = plans(levels, species)
    padded = (plan.whole + 1) * LANES
    slots = devices * CAP
    return pl.pallas_call(
        functools.partial(gather_kernel, plan, devices, (2, 2, 1)),
        out_shape=(
            jax.ShapeDtypeStruct((devices * plan.rows, LANES), F32),
            jax.ShapeDtypeStruct((pieces, columns), BF),
            jax.ShapeDtypeStruct((slots, pieces), BF),
        ),
        in_specs=[HBM] * 6,
        out_specs=(VMEM, VMEM, VMEM),
        scratch_shapes=[
            pltpu.VMEM((species, levels, columns), F32),
            pltpu.SemaphoreType.DMA((species + 4,)),
            pltpu.VMEM((1, columns), F32),
            pltpu.VMEM((1, columns), jnp.int32),
            pltpu.VMEM((1, pieces), jnp.int32),
            pltpu.VMEM((1, pieces), jnp.int32),
            pltpu.VMEM((2 * species * up_to(levels, 16) + 16, columns), BF),
            pltpu.VMEM((padded, 2 * pieces), BF),
        ],
        compiler_params=params(34),
        name="gather_pieces",
    )(*map(in_hbm, (thermal, gas, weight_row, segment_row, target_row, box_row)))


def radiate_call(arrived, opacity, fraction, levels, cells):
    absorbers, points = opacity.shape
    species = absorbers + 1
    devices = lax.axis_size(AXES)
    plan, back = plans(levels, species)
    padded = (plan.whole + 1) * LANES
    slots = devices * CAP
    block = up_to(levels, LEVELS)
    return pl.pallas_call(
        functools.partial(radiate_kernel, plan, back, devices, levels, cells),
        out_shape=jax.ShapeDtypeStruct((devices * back.rows, LANES), F32),
        in_specs=[VMEM, HBM, HBM],
        out_specs=VMEM,
        scratch_shapes=[
            pltpu.VMEM((absorbers, points), F32),
            pltpu.VMEM((1, points), F32),
            pltpu.SemaphoreType.DMA((2,)),
            pltpu.VMEM((2 * slots, padded), BF),
            pltpu.VMEM((slots, 2 * cells), BF),
            pltpu.VMEM((block, cells), F32),
            pltpu.VMEM((block // LEVELS, 4 * absorbers * LEVELS, cells), BF),
            pltpu.VMEM((block, cells), F32),
            pltpu.VMEM((2 * LANES, 2 * cells), BF),
            pltpu.VMEM((levels, points, cells), F32),
            pltpu.VMEM((cells // LANES, 8 * levels, LANES), F32),
        ],
        compiler_params=params(28),
        name="radiate_cells",
    )(arrived, in_hbm(opacity), in_hbm(fraction))


def spread_call(returned, ones, slot, levels):
    pieces, columns = ones.shape
    slots = slot.shape[0]
    devices = slots // CAP
    _, back = plans(levels, 1)
    chunks = 4
    return pl.pallas_call(
        functools.partial(spread_kernel, back, devices, levels, chunks),
        out_shape=jax.ShapeDtypeStruct((levels, columns), F32),
        in_specs=[VMEM, VMEM, VMEM],
        out_specs=HBM,
        scratch_shapes=[
            pltpu.VMEM((slots, 2 * LANES), F32),
            pltpu.VMEM((levels, columns), F32),
            pltpu.SemaphoreType.DMA((chunks,)),
        ],
        compiler_params=params(16),
        name="spread_heat",
    )(returned, ones, slot)


def exchange(value):
    devices = lax.axis_size(AXES)
    chunks = value.reshape(devices, 1, value.size // devices)
    return lax.all_to_all(chunks, AXES, split_axis=0, concat_axis=0, tiled=True).reshape(value.shape)


def shards(thermal, gas, footprint, segment, holder, box, opacity, fraction):
    levels, columns = thermal.shape
    pieces = box.shape[0]
    outgoing, ones, slot = gather_call(
        thermal,
        gas.transpose(1, 0, 2),
        footprint.reshape(1, columns),
        segment.reshape(1, columns),
        holder.reshape(1, pieces),
        box.reshape(1, pieces),
    )
    arrived = exchange(outgoing)
    heat = radiate_call(arrived, opacity.T, fraction.reshape(1, -1), levels, columns // 8)
    returned = exchange(heat)
    return spread_call(returned, ones, slot, levels)


def solution(mesh):
    placed = (
        P(None, AXES),
        P(None, None, AXES),
        P(AXES),
        P(AXES),
        P(AXES, None),
        P(AXES),
        P(),
        P(),
    )
    return jax.shard_map(shards, mesh=mesh, in_specs=placed, out_specs=P(None, AXES), check_vma=False)
```

time: 86.2 us -> 82.7 us (0.959)
  Pallas kernels: 18.4 us -> 14.8 us
    pallas_call x1, Pallas kernels: 7.36 us -> 5.11 us  [radiate_call(): pl.pallas_call(functools.partial(radiate_kernel, plan, back, devices, lev...]
    pallas_call x2, Pallas kernels: 11.1 us -> 9.74 us  [the longest x1 7.58 us: gather_call(): pl.pallas_call(functools.partial(gather_kernel, plan, devices, (2, 2, 1))...]
where the time goes in v2:
time: 82.7 us; the launch traced here: 82.5 us
  blocking collectives  67.7 us (82%)
  Pallas kernels  14.8 us (18%)
    all_to_all x2, blocking collectives, exchange(): lax.all_to_all(chunks, AXES, split_axis=0, concat_axis=0, tiled=True)  67.7 us
    pallas_call x1, Pallas kernels, gather_call(): pl.pallas_call(functools.partial(gather_kernel, plan, devices, (2, 2, 1))...  7.58 us
    pallas_call x1, Pallas kernels, radiate_call(): pl.pallas_call(functools.partial(radiate_kernel, plan, back, devices, lev...  5.11 us
    pallas_call x1, Pallas kernels, spread_call(): pl.pallas_call(functools.partial(spread_kernel, back, devices, levels, ch...  2.16 us

profile of v2, /device:TPU:1, one launch (start us, length us, event | category | flops | bytes accessed | tf_op | source)
XLA Modules:
  0.0 82.5 jit_solution(8040982968867144013)
XLA Ops:
  0.0 7.6 %gather_pieces.1 = (f32[5504,128]{1,0:T(8,128)S(1)}, bf16[512,2048]{1,0:T(8,128)(2,1)S(1)}, bf16[1024,512]{1,0:T(8,128)(2,1)S(1)}) custom-call(f32[137,2048]{1,0:T(8,128)} %thermal.1, f32[137,4,2048]{2,1,0:T(4,128)} %bitcast.15, f32[1,2048]{1,0:T(1,128)} %bitcast.16, s32[1,2048]{1,0:T(1,128)} %bitcast.17, s32[1,512]{1,0:T(1,128)} %bitcast.18, s32[1,512]{1,0:T(1,128)} %bitcast.19), custom_call_target="tpu_custom_call" | custom-call | tf_op jit(solution)/shard_map/gather_pieces/pallas_call | solution.py:336
  7.6 49.5 %all_to_all.10 = f32[128,1,5504]{2,1,0:T(1,128)S(1)} all-to-all(f32[128,1,5504]{2,1,0:T(1,128)S(1)} %bitcast.12), channel_id=1, replica_groups=mesh['dyn'=32,'rad'=4] {'dyn','rad'}, dimensions={0} | all-to-all | bytes 5636096 | tf_op jit(solution)/shard_map/all_to_all | solution.py:415
  57.1 5.1 %radiate_cells.1 = f32[1152,128]{1,0:T(8,128)S(1)} custom-call(f32[5504,128]{1,0:T(8,128)S(1)} %bitcast.11, f32[4,32]{1,0:T(4,128)} %bitcast.20, f32[1,32]{1,0:T(1,128)} %bitcast.21), custom_call_target="tpu_custom_call" | custom-call | tf_op jit(solution)/shard_map/radiate_cells/pallas_call | solution.py:368
  62.2 18.1 %all_to_all.11 = f32[128,1,1152]{2,1,0:T(1,128)S(1)} all-to-all(f32[128,1,1152]{2,1,0:T(1,128)S(1)} %bitcast.14), channel_id=1, replica_groups=mesh['dyn'=32,'rad'=4] {'dyn','rad'}, dimensions={0} | all-to-all | bytes 1179648 | tf_op jit(solution)/shard_map/all_to_all | solution.py:415
  80.4 2.2 %spread_heat.1 = f32[137,2048]{1,0:T(8,128)} custom-call(f32[1152,128]{1,0:T(8,128)S(1)} %bitcast.13, bf16[512,2048]{1,0:T(8,128)(2,1)S(1)} %get-tuple-element.9.ones, bf16[1024,512]{1,0:T(8,128)(2,1)S(1)} %get-tuple-element.10.slot), custom_call_target="tpu_custom_call" | custom-call | tf_op jit(solution)/shard_map/spread_heat/pallas_call | solution.py:397

commit v3 on v2

--- a/solution.py
+++ b/solution.py
@@ -15,6 +15,7 @@
 NT = (((1,), (1,)), ((), ()))
 NN = (((1,), (0,)), ((), ()))
 MIB = 1024 * 1024
+FIRST = 2
 LEVELS = 16
 LOG2E = 1.4426950408889634
 
@@ -59,10 +60,6 @@
     owner = lax.broadcasted_iota(jnp.int32, (devices, pieces), 0) == target
     for s in range(CAP):
         store(s, mask_to(owner & (rank == s)))
-
-
-def piece_rows(segment, pieces):
-    return mask_to(lax.broadcasted_iota(jnp.int32, (pieces, segment.shape[1]), 0) == segment)
 
 
 class Plan:
@@ -103,62 +100,57 @@
         return pltpu.roll(value, LANES - shift, 1) if shift else value
 
 
-def gather_kernel(plan, devices, groups, thermal, gas, weight_in, segment_in, target_in, box_in, out, ones, slot, buf, sems, weight, segment, target, box, left, comp):
+def gather_kernel(plan, devices, groups, late, thermal, gas, weight_in, segment_in, target_in, box_in, out, ones, slot, buf, sems, weight, segment, target, box, left, comp):
     species, levels, columns = buf.shape
     pieces = target.shape[1]
     block = up_to(levels, 16)
-    small = [(target_in, target), (segment_in, segment), (weight_in, weight), (box_in, box)]
+    small = [(segment_in, segment), (weight_in, weight), (target_in, target), (box_in, box)]
     rows = [pltpu.make_async_copy(a, b, sems.at[species + n]) for n, (a, b) in enumerate(small)]
     for copy in rows:
         copy.start()
     copies = [pltpu.make_async_copy(thermal, buf.at[0], sems.at[0])]
     copies += [pltpu.make_async_copy(gas.at[:, k, :], buf.at[k + 1], sems.at[k + 1]) for k in range(species - 1)]
-    for copy in copies:
+    for copy in copies[:FIRST]:
         copy.start()
-    rows[0].wait()
-    owner = target[...]
-    rank = slots_of(owner, devices)
-
-    def store(s, value):
-        slot[s * devices : (s + 1) * devices, :] = value
-
-    slot_rows(owner, rank, devices, store)
-    rows[1].wait()
-    ones[...] = piece_rows(segment[...], pieces)
-    rows[2].wait()
-    rows[3].wait()
+    for copy in rows:
+        copy.wait()
+    for copy in copies[FIRST:]:
+        copy.start()
+    down = jnp.transpose(jnp.broadcast_to(segment[...], (LANES, columns)))
+    for k in range(pieces // LANES):
+        lane = lax.broadcasted_iota(jnp.int32, (columns, LANES), 1) + k * LANES
+        ones[:, k * LANES : (k + 1) * LANES] = mask_to(down == lane)
     w = weight[...]
-    total = species * levels
     end = 2 * species * block
     pair = parts_of(jnp.broadcast_to(w, (8, columns)), 2)
     left[end:, :] = jnp.concatenate([part.astype(F32) for part in pair], axis=0).astype(BF)
+
+    def place():
+        owner = target[...]
+        rank = slots_of(owner, devices)
+
+        def store(s, value):
+            slot[s * devices : (s + 1) * devices, :] = value
+
+        slot_rows(owner, rank, devices, store)
 
     def load(k):
         copies[k].wait()
         for n, part in enumerate(parts_of(buf[k] * w, 2)):
             left[(2 * k + n) * block : (2 * k + n) * block + levels, :] = part
 
-    def keep(first, rows, values):
-        for n, part in enumerate(parts_of(values, 2)):
-            comp[first : first + rows, n * pieces : (n + 1) * pieces] = part
-
-    bounds = [sum(groups[:n]) for n in range(len(groups) + 1)]
-    for begin, stop in zip(bounds, bounds[1:]):
-        last = stop == species
-        for k in range(begin, stop):
-            load(k)
-        sums = dot(left[2 * begin * block : end + 16 if last else 2 * stop * block, :], ones[...], NT)
-        for k in range(begin, stop):
-            a = 2 * (k - begin) * block
-            keep(k * levels, levels, sums[a : a + levels] + sums[a + block : a + block + levels])
-        if last:
-            a = 2 * (stop - begin) * block
-            row = lax.broadcasted_iota(jnp.int32, (comp.shape[0] - total, pieces), 0)
-            held = sums[a : a + 1] + sums[a + 8 : a + 9]
-            keep(total, comp.shape[0] - total, jnp.where(row == 0, held, jnp.where(row == 1, box[...].astype(F32), 0.0)))
+    even = levels // 8 * 8
+    spare = species * even
+
+    def keep(k, sums, a):
+        pair = sums[a : a + levels] + sums[a + block : a + block + levels]
+        comp[k * even : (k + 1) * even, :] = pair[:even]
+        return pair[even:]
+
     wide = 2 * LANES
-    for k in range(comp.shape[0] // wide):
-        pair = [comp[k * wide : (k + 1) * wide, n * pieces : (n + 1) * pieces] for n in range(2)]
+
+    def emit(k):
+        pair = parts_of(comp[k * wide : (k + 1) * wide, :], 2)
         acc = dot(slot[...], pair[0], NT) + dot(slot[...], pair[1], NT)
         for h in range(2):
             tile = 2 * k + h
@@ -169,6 +161,33 @@
             else:
                 for j, value in enumerate(plan.pack(values)):
                     out[pl.ds(CAP * tile + j, devices, stride=plan.rows), :] = value
+
+    emitted = 0
+    ends = []
+    bounds = [sum(groups[:n]) for n in range(len(groups) + 1)]
+    for begin, stop in zip(bounds, bounds[1:]):
+        last = stop == species
+        for k in range(begin, stop):
+            load(k)
+        if begin == 0:
+            place()
+        sums = dot(left[2 * begin * block : end + 16 if last else 2 * stop * block, :], ones[...], NN)
+        for k in range(begin, stop):
+            a = 2 * (k - begin) * block
+            ends.append(keep(k, sums, a))
+        if last:
+            a = 2 * (stop - begin) * block
+            ends.append(sums[a : a + 1] + sums[a + 8 : a + 9])
+            ends.append(box[...].astype(F32))
+            row = lax.broadcasted_iota(jnp.int32, (comp.shape[0] - spare, pieces), 0)
+            rest = jnp.zeros(row.shape, F32)
+            for n, value in enumerate(ends):
+                rest = jnp.where(row == n, value, rest)
+            comp[spare:, :] = rest
+        ready = comp.shape[0] if last or late else stop * even
+        while (emitted + 1) * wide <= ready and (last or not late):
+            emit(emitted)
+            emitted += 1
 
 
 def as_column(row, width):
@@ -252,14 +271,21 @@
     turned = mask_to(lax.broadcasted_iota(jnp.int32, (cells, slots), 0) == cell_row)
     sums = jnp.transpose(dot(jnp.concatenate([turned, turned], axis=1), parts[...], NN))
     inverse = 1.0 / jnp.maximum(sums[fields - 2 : fields - 1, :], 1.0)
-    warm = sums[0:levels] * inverse
+    even = levels // 8 * 8
+    block = mean.shape[0]
+    spare = (absorbers + 1) * even
+
+    def means(k):
+        row = lax.broadcasted_iota(jnp.int32, (block - even, cells), 0)
+        mean[0:even, :] = sums[k * even : (k + 1) * even] * inverse
+        mean[even:, :] = jnp.where(row == 0, sums[spare + k : spare + k + 1] * inverse, 0.0)
+        return mean[...]
+
+    warm = means(0)
     square = warm * warm
-    t4[0:levels, :] = square * square
-    block = mean.shape[0]
-    mean[levels:, :] = jnp.zeros((block - levels, cells), F32)
+    t4[...] = square * square
     for a in range(absorbers):
-        mean[0:levels, :] = sums[(a + 1) * levels : (a + 2) * levels] * inverse
-        for n, part in enumerate(parts_of(mean[...], 2)):
+        for n, part in enumerate(parts_of(means(a + 1), 2)):
             for m in range(2):
                 first = ((2 * m + n) * absorbers + a) * LEVELS
                 for b in range(block // LEVELS):
@@ -300,7 +326,7 @@
     copies = []
     for c in range(chunks):
         own = slice(c * size, (c + 1) * size)
-        value = dot(both, ones[:, own], NN)
+        value = dot(both, ones[own, :], NT)
         held[:, own] = value[:rows] + value[block : block + rows]
         copies.append(pltpu.make_async_copy(held.at[:, own], out.at[:, own], sems.at[c]))
         copies[-1].start()
@@ -334,10 +360,10 @@
     padded = (plan.whole + 1) * LANES
     slots = devices * CAP
     return pl.pallas_call(
-        functools.partial(gather_kernel, plan, devices, (2, 2, 1)),
+        functools.partial(gather_kernel, plan, devices, (1, 1, 1, 1, 1), True),
         out_shape=(
             jax.ShapeDtypeStruct((devices * plan.rows, LANES), F32),
-            jax.ShapeDtypeStruct((pieces, columns), BF),
+            jax.ShapeDtypeStruct((columns, pieces), BF),
             jax.ShapeDtypeStruct((slots, pieces), BF),
         ),
         in_specs=[HBM] * 6,
@@ -350,7 +376,7 @@
             pltpu.VMEM((1, pieces), jnp.int32),
             pltpu.VMEM((1, pieces), jnp.int32),
             pltpu.VMEM((2 * species * up_to(levels, 16) + 16, columns), BF),
-            pltpu.VMEM((padded, 2 * pieces), BF),
+            pltpu.VMEM((padded, pieces), F32),
         ],
         compiler_params=params(34),
         name="gather_pieces",
@@ -389,7 +415,7 @@
 
 
 def spread_call(returned, ones, slot, levels):
-    pieces, columns = ones.shape
+    columns, pieces = ones.shape
     slots = slot.shape[0]
     devices = slots // CAP
     _, back = plans(levels, 1)

time: 82.7 us -> 82.3 us (level)
  no operation moved by 1% of the time
where the time goes in v3:
time: 82.3 us; the launch traced here: 82.1 us
  blocking collectives  67.6 us (82%)
  Pallas kernels  14.5 us (18%)
    all_to_all x2, blocking collectives, exchange(): lax.all_to_all(chunks, AXES, split_axis=0, concat_axis=0, tiled=True)  67.6 us
    pallas_call x1, Pallas kernels, gather_call(): pl.pallas_call(functools.partial(gather_kernel, plan, devices, (1, 1, 1,...  7.21 us
    pallas_call x1, Pallas kernels, radiate_call(): pl.pallas_call(functools.partial(radiate_kernel, plan, back, devices, lev...  5.11 us
    pallas_call x1, Pallas kernels, spread_call(): pl.pallas_call(functools.partial(spread_kernel, back, devices, levels, ch...  2.16 us

profile of v3, /device:TPU:1, one launch (start us, length us, event | category | flops | bytes accessed | tf_op | source)
XLA Modules:
  0.0 82.1 jit_solution(2411998773528349297)
XLA Ops:
  0.0 7.2 %gather_pieces.1 = (f32[5504,128]{1,0:T(8,128)S(1)}, bf16[2048,512]{1,0:T(8,128)(2,1)S(1)}, bf16[1024,512]{1,0:T(8,128)(2,1)S(1)}) custom-call(f32[137,2048]{1,0:T(8,128)} %thermal.1, f32[137,4,2048]{2,1,0:T(4,128)} %bitcast.15, f32[1,2048]{1,0:T(1,128)} %bitcast.16, s32[1,2048]{1,0:T(1,128)} %bitcast.17, s32[1,512]{1,0:T(1,128)} %bitcast.18, s32[1,512]{1,0:T(1,128)} %bitcast.19), custom_call_target="tpu_custom_call" | custom-call | tf_op jit(solution)/shard_map/gather_pieces/pallas_call | solution.py:362
  7.2 49.5 %all_to_all.10 = f32[128,1,5504]{2,1,0:T(1,128)S(1)} all-to-all(f32[128,1,5504]{2,1,0:T(1,128)S(1)} %bitcast.12), channel_id=1, replica_groups=mesh['dyn'=32,'rad'=4] {'dyn','rad'}, dimensions={0} | all-to-all | bytes 5636096 | tf_op jit(solution)/shard_map/all_to_all | solution.py:441
  56.7 5.1 %radiate_cells.1 = f32[1152,128]{1,0:T(8,128)S(1)} custom-call(f32[5504,128]{1,0:T(8,128)S(1)} %bitcast.11, f32[4,32]{1,0:T(4,128)} %bitcast.20, f32[1,32]{1,0:T(1,128)} %bitcast.21), custom_call_target="tpu_custom_call" | custom-call | tf_op jit(solution)/shard_map/radiate_cells/pallas_call | solution.py:394
  61.8 18.1 %all_to_all.11 = f32[128,1,1152]{2,1,0:T(1,128)S(1)} all-to-all(f32[128,1,1152]{2,1,0:T(1,128)S(1)} %bitcast.14), channel_id=1, replica_groups=mesh['dyn'=32,'rad'=4] {'dyn','rad'}, dimensions={0} | all-to-all | bytes 1179648 | tf_op jit(solution)/shard_map/all_to_all | solution.py:441
  80.0 2.2 %spread_heat.1 = f32[137,2048]{1,0:T(8,128)} custom-call(f32[1152,128]{1,0:T(8,128)S(1)} %bitcast.13, bf16[2048,512]{1,0:T(8,128)(2,1)S(1)} %get-tuple-element.9.ones, bf16[1024,512]{1,0:T(8,128)(2,1)S(1)} %get-tuple-element.10.slot), custom_call_target="tpu_custom_call" | custom-call | tf_op jit(solution)/shard_map/spread_heat/pallas_call | solution.py:423

commit v4 on v3

--- a/solution.py
+++ b/solution.py
@@ -16,6 +16,7 @@
 NN = (((1,), (0,)), ((), ()))
 MIB = 1024 * 1024
 FIRST = 2
+BATCHES = {0: 2, 2: 5}
 LEVELS = 16
 LOG2E = 1.4426950408889634
 
@@ -135,7 +136,9 @@
         slot_rows(owner, rank, devices, store)
 
     def load(k):
-        copies[k].wait()
+        if k in BATCHES:
+            for copy in copies[k : BATCHES[k]]:
+                copy.wait()
         for n, part in enumerate(parts_of(buf[k] * w, 2)):
             left[(2 * k + n) * block : (2 * k + n) * block + levels, :] = part
 
@@ -210,35 +213,56 @@
     return jnp.concatenate([jnp.where(level == i, held, 0.0) for i in range(LEVELS)], axis=0).astype(BF)
 
 
-def sweep(depths, xs, t4, frac, lost, gain, levels, cells):
+def sweep(depths, xs, rise, first, frac, kept, below, above, levels, cells):
     points = frac.shape[0]
-    halves = gain.shape[0]
-
-    def fold(value):
-        return jnp.sum(value.reshape(points // 8, 8, cells), axis=0)
-
-    flux = jnp.zeros((points, cells), F32)
+    halves = below.shape[0]
+
+    def hold(ref, l, value):
+        part = jnp.sum(value.reshape(points // 8, 8, cells), axis=0)
+        for h in range(halves):
+            ref[h, 8 * l : 8 * l + 8, :] = part[:, h * LANES : (h + 1) * LANES]
+
+    lack = frac * first
+    through = lack
     for b in range(up_to(levels, LEVELS) // LEVELS):
-        take = 1.0 - jnp.exp2(dot(depths, xs[b], NN))
+        trans = jnp.exp2(dot(depths, xs[b], NN))
         for i in range(min(LEVELS, levels - b * LEVELS)):
             l = b * LEVELS + i
-            own = take[i * points : (i + 1) * points]
-            lost[l] = own
-            step = own * (frac * t4[l : l + 1, :] - flux)
-            part = fold(step)
-            for h in range(halves):
-                gain[h, 8 * l : 8 * l + 8, :] = part[:, h * LANES : (h + 1) * LANES]
-            flux = flux + step
-    flux = 0.95 * (frac * t4[levels - 1 : levels, :]) + 0.05 * flux
+            own = trans[i * points : (i + 1) * points]
+            kept[l] = own
+            through = own * lack
+            hold(below, l, through)
+            if l + 1 < levels:
+                lack = through + frac * rise[l : l + 1, :]
+    lack = 0.05 * through
     for l in range(levels - 1, -1, -1):
-        step = lost[l] * (frac * t4[l : l + 1, :] - flux)
-        part = fold(step)
-        for h in range(halves):
-            gain[h, 8 * l : 8 * l + 8, :] += part[:, h * LANES : (h + 1) * LANES]
-        flux = flux + step
-
-
-def radiate_kernel(plan, back, devices, levels, cells, arrived, opacity_in, fraction_in, out, opacity, fraction, sems, parts, match, mean, xs, t4, heat, lost, gain):
+        through = kept[l] * lack
+        hold(above, l, through)
+        if l:
+            lack = through - frac * rise[l - 1 : l, :]
+
+
+def taken(below, above, rise, first, frac, enter, h, levels):
+    lanes = slice(h * LANES, (h + 1) * LANES)
+
+    def total(ref):
+        value = ref[h, pl.ds(0, levels, stride=8), :]
+        for g in range(1, 8):
+            value = value + ref[h, pl.ds(g, levels, stride=8), :]
+        return value
+
+    down, up = total(below), total(above)
+    weight = jnp.sum(frac[:, lanes], axis=0, keepdims=True)
+    change = weight * rise[0 : levels - 1, lanes]
+    enter[0:1, :] = weight * first[:, lanes]
+    enter[1:levels, :] = down[: levels - 1] + change
+    value = enter[0:levels, :] - down
+    enter[0 : levels - 1, :] = up[1:] - change
+    enter[levels - 1 : levels, :] = 0.05 * down[levels - 1 :]
+    return value + (enter[0:levels, :] - up)
+
+
+def radiate_kernel(plan, back, devices, levels, cells, arrived, opacity_in, fraction_in, out, opacity, fraction, sems, parts, match, mean, xs, t4, rise, heat, kept, below, above, enter):
     copies = [
         pltpu.make_async_copy(opacity_in, opacity, sems.at[0]),
         pltpu.make_async_copy(fraction_in, fraction, sems.at[1]),
@@ -284,6 +308,7 @@
     warm = means(0)
     square = warm * warm
     t4[...] = square * square
+    rise[0 : levels - 1, :] = t4[1:levels, :] - t4[0 : levels - 1, :]
     for a in range(absorbers):
         for n, part in enumerate(parts_of(means(a + 1), 2)):
             for m in range(2):
@@ -293,12 +318,11 @@
     for copy in copies:
         copy.wait()
     frac = as_column(fraction[...], cells)
-    sweep(depth_matrix(opacity, points), xs, t4, frac, lost, gain, levels, cells)
+    top = t4[0:1, :]
+    sweep(depth_matrix(opacity, points), xs, rise, top, frac, kept, below, above, levels, cells)
     heat[...] = jnp.zeros(heat.shape, BF)
-    for h in range(gain.shape[0]):
-        total = gain[h, pl.ds(0, levels, stride=8), :]
-        for g in range(1, 8):
-            total = total + gain[h, pl.ds(g, levels, stride=8), :]
+    for h in range(below.shape[0]):
+        total = taken(below, above, rise, top, frac, enter, h, levels)
         for n, part in enumerate(parts_of(-total, 2)):
             first = n * cells + h * LANES
             heat[0:levels, first : first + LANES] = part
@@ -360,7 +384,7 @@
     padded = (plan.whole + 1) * LANES
     slots = devices * CAP
     return pl.pallas_call(
-        functools.partial(gather_kernel, plan, devices, (1, 1, 1, 1, 1), True),
+        functools.partial(gather_kernel, plan, devices, (2, 3), True),
         out_shape=(
             jax.ShapeDtypeStruct((devices * plan.rows, LANES), F32),
             jax.ShapeDtypeStruct((columns, pieces), BF),
@@ -405,9 +429,12 @@
             pltpu.VMEM((block, cells), F32),
             pltpu.VMEM((block // LEVELS, 4 * absorbers * LEVELS, cells), BF),
             pltpu.VMEM((block, cells), F32),
+            pltpu.VMEM((block, cells), F32),
             pltpu.VMEM((2 * LANES, 2 * cells), BF),
             pltpu.VMEM((levels, points, cells), F32),
             pltpu.VMEM((cells // LANES, 8 * levels, LANES), F32),
+            pltpu.VMEM((cells // LANES, 8 * levels, LANES), F32),
+            pltpu.VMEM((block, LANES), F32),
         ],
         compiler_params=params(28),
         name="radiate_cells",

time: 82.3 us -> 81.7 us (level)
  no operation moved by 1% of the time
where the time goes in v4:
time: 81.7 us; the launch traced here: 81.6 us
  blocking collectives  67.7 us (83%)
  Pallas kernels  13.9 us (17%)
    all_to_all x2, blocking collectives, exchange(): lax.all_to_all(chunks, AXES, split_axis=0, concat_axis=0, tiled=True)  67.7 us
    pallas_call x1, Pallas kernels, gather_call(): pl.pallas_call(functools.partial(gather_kernel, plan, devices, (2, 3), Tr...  6.98 us
    pallas_call x1, Pallas kernels, radiate_call(): pl.pallas_call(functools.partial(radiate_kernel, plan, back, devices, lev...  4.73 us
    pallas_call x1, Pallas kernels, spread_call(): pl.pallas_call(functools.partial(spread_kernel, back, devices, levels, ch...  2.15 us

profile of v4, /device:TPU:1, one launch (start us, length us, event | category | flops | bytes accessed | tf_op | source)
XLA Modules:
  0.0 81.6 jit_solution(8935044385279761936)
XLA Ops:
  0.0 7.0 %gather_pieces.1 = (f32[5504,128]{1,0:T(8,128)S(1)}, bf16[2048,512]{1,0:T(8,128)(2,1)S(1)}, bf16[1024,512]{1,0:T(8,128)(2,1)S(1)}) custom-call(f32[137,2048]{1,0:T(8,128)} %thermal.1, f32[137,4,2048]{2,1,0:T(4,128)} %bitcast.15, f32[1,2048]{1,0:T(1,128)} %bitcast.16, s32[1,2048]{1,0:T(1,128)} %bitcast.17, s32[1,512]{1,0:T(1,128)} %bitcast.18, s32[1,512]{1,0:T(1,128)} %bitcast.19), custom_call_target="tpu_custom_call" | custom-call | tf_op jit(solution)/shard_map/gather_pieces/pallas_call | solution.py:386
  7.0 49.5 %all_to_all.10 = f32[128,1,5504]{2,1,0:T(1,128)S(1)} all-to-all(f32[128,1,5504]{2,1,0:T(1,128)S(1)} %bitcast.12), channel_id=1, replica_groups=mesh['dyn'=32,'rad'=4] {'dyn','rad'}, dimensions={0} | all-to-all | bytes 5636096 | tf_op jit(solution)/shard_map/all_to_all | solution.py:468
  56.5 4.7 %radiate_cells.1 = f32[1152,128]{1,0:T(8,128)S(1)} custom-call(f32[5504,128]{1,0:T(8,128)S(1)} %bitcast.11, f32[4,32]{1,0:T(4,128)} %bitcast.20, f32[1,32]{1,0:T(1,128)} %bitcast.21), custom_call_target="tpu_custom_call" | custom-call | tf_op jit(solution)/shard_map/radiate_cells/pallas_call | solution.py:418
  61.3 18.1 %all_to_all.11 = f32[128,1,1152]{2,1,0:T(1,128)S(1)} all-to-all(f32[128,1,1152]{2,1,0:T(1,128)S(1)} %bitcast.14), channel_id=1, replica_groups=mesh['dyn'=32,'rad'=4] {'dyn','rad'}, dimensions={0} | all-to-all | bytes 1179648 | tf_op jit(solution)/shard_map/all_to_all | solution.py:468
  79.4 2.2 %spread_heat.1 = f32[137,2048]{1,0:T(8,128)} custom-call(f32[1152,128]{1,0:T(8,128)S(1)} %bitcast.13, bf16[2048,512]{1,0:T(8,128)(2,1)S(1)} %get-tuple-element.9.ones, bf16[1024,512]{1,0:T(8,128)(2,1)S(1)} %get-tuple-element.10.slot), custom_call_target="tpu_custom_call" | custom-call | tf_op jit(solution)/shard_map/spread_heat/pallas_call | solution.py:450

commit v5 on v4

--- a/solution.py
+++ b/solution.py
@@ -275,23 +275,20 @@
     absorbers, points = opacity.shape
     tails = [arrived[pl.ds(CAP * plan.whole + j, devices, stride=plan.rows), :] for j in range(plan.tail)]
     pick = mask_to(lax.broadcasted_iota(jnp.int32, (8, LANES), 1) == lane - 1)
-    rows = []
     for s in range(CAP):
         for k in range(plan.whole + 1):
             if k < plan.whole:
                 value = arrived[pl.ds(CAP * k + s, devices, stride=plan.rows), :]
             else:
                 value = plan.unpack(tails, s)
-            split = parts_of(value, 2)
-            for n, part in enumerate(split):
+            for n, part in enumerate(parts_of(value, 2)):
                 first = n * slots + s * devices
                 parts[first : first + devices, k * LANES : (k + 1) * LANES] = part
         cell = value[:, lane - 1 : lane].astype(jnp.int32)
         here = mask_to(cell == lax.broadcasted_iota(jnp.int32, (devices, cells), 1))
         for n in range(2):
             match[s * devices : (s + 1) * devices, n * cells : (n + 1) * cells] = here
-        rows.append(dot(pick, split[0], NT)[0:1])
-    cell_row = jnp.concatenate(rows, axis=1).astype(jnp.int32)
+    cell_row = dot(pick, parts[0:slots, plan.whole * LANES :], NT)[0:1].astype(jnp.int32)
     turned = mask_to(lax.broadcasted_iota(jnp.int32, (cells, slots), 0) == cell_row)
     sums = jnp.transpose(dot(jnp.concatenate([turned, turned], axis=1), parts[...], NN))
     inverse = 1.0 / jnp.maximum(sums[fields - 2 : fields - 1, :], 1.0)

time: 81.7 us -> 81.8 us (level)
  no operation moved by 1% of the time
where the time goes in v5:
time: 81.8 us; the launch traced here: 81.6 us
  blocking collectives  67.7 us (83%)
  Pallas kernels  14 us (17%)
    all_to_all x2, blocking collectives, exchange(): lax.all_to_all(chunks, AXES, split_axis=0, concat_axis=0, tiled=True)  67.7 us
    pallas_call x1, Pallas kernels, gather_call(): pl.pallas_call(functools.partial(gather_kernel, plan, devices, (2, 3), Tr...  6.98 us
    pallas_call x1, Pallas kernels, radiate_call(): pl.pallas_call(functools.partial(radiate_kernel, plan, back, devices, lev...  4.81 us
    pallas_call x1, Pallas kernels, spread_call(): pl.pallas_call(functools.partial(spread_kernel, back, devices, levels, ch...  2.16 us

profile of v5, /device:TPU:1, one launch (start us, length us, event | category | flops | bytes accessed | tf_op | source)
XLA Modules:
  0.0 81.6 jit_solution(2006696547872547527)
XLA Ops:
  0.0 7.0 %gather_pieces.1 = (f32[5504,128]{1,0:T(8,128)S(1)}, bf16[2048,512]{1,0:T(8,128)(2,1)S(1)}, bf16[1024,512]{1,0:T(8,128)(2,1)S(1)}) custom-call(f32[137,2048]{1,0:T(8,128)} %thermal.1, f32[137,4,2048]{2,1,0:T(4,128)} %bitcast.15, f32[1,2048]{1,0:T(1,128)} %bitcast.16, s32[1,2048]{1,0:T(1,128)} %bitcast.17, s32[1,512]{1,0:T(1,128)} %bitcast.18, s32[1,512]{1,0:T(1,128)} %bitcast.19), custom_call_target="tpu_custom_call" | custom-call | tf_op jit(solution)/shard_map/gather_pieces/pallas_call | solution.py:383
  7.0 49.5 %all_to_all.10 = f32[128,1,5504]{2,1,0:T(1,128)S(1)} all-to-all(f32[128,1,5504]{2,1,0:T(1,128)S(1)} %bitcast.12), channel_id=1, replica_groups=mesh['dyn'=32,'rad'=4] {'dyn','rad'}, dimensions={0} | all-to-all | bytes 5636096 | tf_op jit(solution)/shard_map/all_to_all | solution.py:465
  56.5 4.8 %radiate_cells.1 = f32[1152,128]{1,0:T(8,128)S(1)} custom-call(f32[5504,128]{1,0:T(8,128)S(1)} %bitcast.11, f32[4,32]{1,0:T(4,128)} %bitcast.20, f32[1,32]{1,0:T(1,128)} %bitcast.21), custom_call_target="tpu_custom_call" | custom-call | tf_op jit(solution)/shard_map/radiate_cells/pallas_call | solution.py:415
  61.3 18.1 %all_to_all.11 = f32[128,1,1152]{2,1,0:T(1,128)S(1)} all-to-all(f32[128,1,1152]{2,1,0:T(1,128)S(1)} %bitcast.14), channel_id=1, replica_groups=mesh['dyn'=32,'rad'=4] {'dyn','rad'}, dimensions={0} | all-to-all | bytes 1179648 | tf_op jit(solution)/shard_map/all_to_all | solution.py:465
  79.5 2.2 %spread_heat.1 = f32[137,2048]{1,0:T(8,128)} custom-call(f32[1152,128]{1,0:T(8,128)S(1)} %bitcast.13, bf16[2048,512]{1,0:T(8,128)(2,1)S(1)} %get-tuple-element.9.ones, bf16[1024,512]{1,0:T(8,128)(2,1)S(1)} %get-tuple-element.10.slot), custom_call_target="tpu_custom_call" | custom-call | tf_op jit(solution)/shard_map/spread_heat/pallas_call | solution.py:447

commit v6 on v5

--- a/solution.py
+++ b/solution.py
@@ -286,8 +286,7 @@
                 parts[first : first + devices, k * LANES : (k + 1) * LANES] = part
         cell = value[:, lane - 1 : lane].astype(jnp.int32)
         here = mask_to(cell == lax.broadcasted_iota(jnp.int32, (devices, cells), 1))
-        for n in range(2):
-            match[s * devices : (s + 1) * devices, n * cells : (n + 1) * cells] = here
+        match[s * devices : (s + 1) * devices, :] = here
     cell_row = dot(pick, parts[0:slots, plan.whole * LANES :], NT)[0:1].astype(jnp.int32)
     turned = mask_to(lax.broadcasted_iota(jnp.int32, (cells, slots), 0) == cell_row)
     sums = jnp.transpose(dot(jnp.concatenate([turned, turned], axis=1), parts[...], NN))
@@ -323,7 +322,7 @@
         for n, part in enumerate(parts_of(-total, 2)):
             first = n * cells + h * LANES
             heat[0:levels, first : first + LANES] = part
-    acc = dot(match[...], heat[...], NT)
+    acc = dot(match[...], heat[:, :cells], NT) + dot(match[...], heat[:, cells:], NT)
     for s in range(CAP):
         out[pl.ds(s, devices, stride=back.rows), :] = acc[s * devices : (s + 1) * devices, :LANES]
     rests = [acc[s * devices : (s + 1) * devices, LANES:] for s in range(CAP)]
@@ -422,7 +421,7 @@
             pltpu.VMEM((1, points), F32),
             pltpu.SemaphoreType.DMA((2,)),
             pltpu.VMEM((2 * slots, padded), BF),
-            pltpu.VMEM((slots, 2 * cells), BF),
+            pltpu.VMEM((slots, cells), BF),
             pltpu.VMEM((block, cells), F32),
             pltpu.VMEM((block // LEVELS, 4 * absorbers * LEVELS, cells), BF),
             pltpu.VMEM((block, cells), F32),

time: 81.8 us -> 81.8 us (level)
  no operation moved by 1% of the time
where the time goes in v6:
time: 81.8 us; the launch traced here: 81.7 us
  blocking collectives  67.7 us (83%)
  Pallas kernels  14 us (17%)
    all_to_all x2, blocking collectives, exchange(): lax.all_to_all(chunks, AXES, split_axis=0, concat_axis=0, tiled=True)  67.7 us
    pallas_call x1, Pallas kernels, gather_call(): pl.pallas_call(functools.partial(gather_kernel, plan, devices, (2, 3), Tr...  6.98 us
    pallas_call x1, Pallas kernels, radiate_call(): pl.pallas_call(functools.partial(radiate_kernel, plan, back, devices, lev...  4.84 us
    pallas_call x1, Pallas kernels, spread_call(): pl.pallas_call(functools.partial(spread_kernel, back, devices, levels, ch...  2.15 us

profile of v6, /device:TPU:1, one launch (start us, length us, event | category | flops | bytes accessed | tf_op | source)
XLA Modules:
  0.0 81.7 jit_solution(7287321756578351326)
XLA Ops:
  0.0 7.0 %gather_pieces.1 = (f32[5504,128]{1,0:T(8,128)S(1)}, bf16[2048,512]{1,0:T(8,128)(2,1)S(1)}, bf16[1024,512]{1,0:T(8,128)(2,1)S(1)}) custom-call(f32[137,2048]{1,0:T(8,128)} %thermal.1, f32[137,4,2048]{2,1,0:T(4,128)} %bitcast.15, f32[1,2048]{1,0:T(1,128)} %bitcast.16, s32[1,2048]{1,0:T(1,128)} %bitcast.17, s32[1,512]{1,0:T(1,128)} %bitcast.18, s32[1,512]{1,0:T(1,128)} %bitcast.19), custom_call_target="tpu_custom_call" | custom-call | tf_op jit(solution)/shard_map/gather_pieces/pallas_call | solution.py:382
  7.0 49.5 %all_to_all.10 = f32[128,1,5504]{2,1,0:T(1,128)S(1)} all-to-all(f32[128,1,5504]{2,1,0:T(1,128)S(1)} %bitcast.12), channel_id=1, replica_groups=mesh['dyn'=32,'rad'=4] {'dyn','rad'}, dimensions={0} | all-to-all | bytes 5636096 | tf_op jit(solution)/shard_map/all_to_all | solution.py:464
  56.5 4.8 %radiate_cells.1 = f32[1152,128]{1,0:T(8,128)S(1)} custom-call(f32[5504,128]{1,0:T(8,128)S(1)} %bitcast.11, f32[4,32]{1,0:T(4,128)} %bitcast.20, f32[1,32]{1,0:T(1,128)} %bitcast.21), custom_call_target="tpu_custom_call" | custom-call | tf_op jit(solution)/shard_map/radiate_cells/pallas_call | solution.py:414
  61.4 18.1 %all_to_all.11 = f32[128,1,1152]{2,1,0:T(1,128)S(1)} all-to-all(f32[128,1,1152]{2,1,0:T(1,128)S(1)} %bitcast.14), channel_id=1, replica_groups=mesh['dyn'=32,'rad'=4] {'dyn','rad'}, dimensions={0} | all-to-all | bytes 1179648 | tf_op jit(solution)/shard_map/all_to_all | solution.py:464
  79.5 2.2 %spread_heat.1 = f32[137,2048]{1,0:T(8,128)} custom-call(f32[1152,128]{1,0:T(8,128)S(1)} %bitcast.13, bf16[2048,512]{1,0:T(8,128)(2,1)S(1)} %get-tuple-element.9.ones, bf16[1024,512]{1,0:T(8,128)(2,1)S(1)} %get-tuple-element.10.slot), custom_call_target="tpu_custom_call" | custom-call | tf_op jit(solution)/shard_map/spread_heat/pallas_call | solution.py:446
